TPU v7x, 512 devices: a whole 4x4x16 slice. The times are simulated.
512 devices in a mesh: gx: 64 (over y, z_lo, core), gy: 8 (over z_hi, x).
Axes of the slice: x: 4, y: 4, z: 16 (z_hi: 2, z_lo: 8; z = z_hi * 8 + z_lo), core: 2. Of those that a mesh axis runs over, the one named last changes fastest.
Arguments:
- grid_field: bfloat16 [2, 1024, 256, 512], P(None, 'gx', 'gy'), may hold values from -6 to 6
- spectral_weight: bfloat16 [128, 2, 512, 512], P('gx', None, None, 'gy'), may hold values from -0.1875 to 0.1875
- skip_weight: bfloat16 [512, 512], replicated, may hold values from -0.25 to 0.25
- inner_weight: bfloat16 [1024, 512], replicated, may hold values from -0.25 to 0.25
- outer_weight: bfloat16 [1024, 512], replicated, may hold values from -0.1875 to 0.1875
Outputs:
- layer_out: bfloat16 [2, 1024, 256, 512], P(None, 'gx', 'gy')
All inputs are finite; a program needn't handle non-finite values.
Results may differ from a plain program's by a relative error of at most 0.0093.
Values may be sent and summed in bfloat16 or wider, within the bound.
A program may use at most 64 MiB of HBM per device.

v0:
```python
import math

import jax
import jax.numpy as jnp
from jax import lax
from jax.sharding import PartitionSpec as P

KX = 16
KY = 8


def cut_along(array, dim, count):
    dims = array.shape
    blocks = array.reshape(*dims[:dim], count, dims[dim] // count, *dims[dim + 1 :])
    return jnp.moveaxis(blocks, dim, 0)


def summed_on_arrival(array, axis, dim):
    count = lax.axis_size(axis)
    blocks = lax.all_to_all(cut_along(array, dim, count), axis, 0, 0, tiled=True)
    return jnp.sum(blocks.astype(jnp.float32), axis=0)


def copy_for_each(array, axis):
    count = lax.axis_size(axis)
    return lax.all_to_all(
        jnp.broadcast_to(array[None], (count, *array.shape)), axis, 0, 0, tiled=True
    )


def taken_together(array, axis):
    return copy_for_each(array, axis).sum(axis=0)


def laid_out(blocks, dim):
    dims = list(blocks.shape[1:])
    dims[dim] *= blocks.shape[0]
    return jnp.moveaxis(blocks, 0, dim).reshape(dims)


def collect(array, axis, dim):
    return laid_out(copy_for_each(array, axis), dim)


def phase_table(row_ids, col_ids, total_rows, total_cols):
    x_modes = jnp.arange(KX, dtype=jnp.int32)
    y_modes = jnp.arange(KY, dtype=jnp.int32)
    x_phase = (x_modes[:, None] * row_ids[None, :] % total_rows).astype(jnp.float32) / total_rows
    y_phase = (y_modes[:, None] * col_ids[None, :] % total_cols).astype(jnp.float32) / total_cols
    angles = (x_phase[:, None, :, None] + y_phase[None, :, None, :]) * (2.0 * math.pi)
    angles = angles.reshape(KX * KY, row_ids.shape[0] * col_ids.shape[0])
    return jnp.concatenate([jnp.cos(angles), -jnp.sin(angles)], axis=0).astype(jnp.bfloat16)


def local(grid_field, spectral_weight, skip_weight, inner_weight, outer_weight):
    micro_count, row_count, col_count, width_count = grid_field.shape
    x_devices = lax.axis_size("gx")
    y_devices = lax.axis_size("gy")
    total_rows = row_count * x_devices
    total_cols = col_count * y_devices
    mode_count = KX * KY
    row_ids = lax.axis_index("gx") * row_count + jnp.arange(row_count, dtype=jnp.int32)
    col_ids = lax.axis_index("gy") * col_count + jnp.arange(col_count, dtype=jnp.int32)
    basis = phase_table(row_ids, col_ids, total_rows, total_cols)
    flat_rows = grid_field.reshape(micro_count, row_count * col_count, width_count)
    partial_value = jnp.einsum("kn,bnc->kbc", basis, flat_rows, preferred_element_type=jnp.float32)
    partial_value = partial_value.reshape(2, mode_count, micro_count, width_count)
    owned_modes = summed_on_arrival(partial_value.astype(jnp.bfloat16), "gx", 1)
    owned_modes = taken_together(owned_modes, "gy")
    spectrum = (owned_modes * (1.0 / math.sqrt(total_rows * total_cols))).astype(jnp.bfloat16)
    weight_re = spectral_weight[:, 0]
    weight_im = spectral_weight[:, 1]
    mixed_re = jnp.einsum(
        "mbc,mcd->mbd", spectrum[0], weight_re, preferred_element_type=jnp.float32
    ) - jnp.einsum("mbc,mcd->mbd", spectrum[1], weight_im, preferred_element_type=jnp.float32)
    mixed_im = jnp.einsum(
        "mbc,mcd->mbd", spectrum[0], weight_im, preferred_element_type=jnp.float32
    ) + jnp.einsum("mbc,mcd->mbd", spectrum[1], weight_re, preferred_element_type=jnp.float32)
    mixed_modes = jnp.stack([mixed_re, mixed_im]).astype(jnp.bfloat16)
    gathered = collect(mixed_modes, "gy", 3)
    gathered = collect(gathered, "gx", 1)
    gathered = gathered.reshape(2 * mode_count, micro_count, width_count)
    spectral = jnp.einsum("kn,kbc->bnc", basis, gathered, preferred_element_type=jnp.float32)
    spectral = spectral * (1.0 / math.sqrt(mode_count))
    skip_term = jnp.einsum(
        "bnc,cd->bnd", flat_rows, skip_weight, preferred_element_type=jnp.float32
    )
    active = jax.nn.gelu(spectral + skip_term).astype(jnp.bfloat16)
    hidden = jax.nn.gelu(
        jnp.einsum("bnc,hc->bnh", active, inner_weight, preferred_element_type=jnp.float32)
    )
    hidden = hidden.astype(jnp.bfloat16)
    feed_forward = jnp.einsum(
        "bnh,hc->bnc", hidden, outer_weight, preferred_element_type=jnp.float32
    )
    layer_out = (active.astype(jnp.float32) + feed_forward).astype(jnp.bfloat16)
    return layer_out.reshape(micro_count, row_count, col_count, width_count)


def solution(mesh):
    in_specs = (P(None, "gx", "gy", None), P("gx", None, None, "gy"), P(), P(), P())
    out_specs = P(None, "gx", "gy", None)
    return jax.shard_map(local, mesh=mesh, in_specs=in_specs, out_specs=out_specs, check_vma=False)
```

profile of v0, /device:TPU:1, one launch (start us, length us, event | category | flops | bytes accessed | tf_op | source)
XLA Modules:
  0.0 148.1 jit_solution(1133912965750387153)
XLA Ops:
  0.0 0.0 copy-start
  0.1 4.1 %cosine_convert_fusion = (bf16[16,8,16,32]{3,2,1,0:T(8,128)(2,1)S(1)}, bf16[16,8,16,32]{3,2,1,0:T(8,128)(2,1)S(1)}) fusion(f32[8,32]{1,0:T(8,128)S(1)} %fusion.44, f32[16,16]{1,0:T(8,128)S(1)} %fusion.38), kind=kLoop, calls=%fused_computation.31 | loop fusion | flops 327680 | bytes 264192 | tf_op jit(solution)/shard_map/convert.7
  4.2 0.4 cos.7
  4.7 0.1 copy.63
  4.8 0.5 neg.7
  5.2 0.1 copy.64
  5.4 0.1 copy.65
  5.6 0.0 copy-done
  5.6 0.4 convolution_convert_fusion
  6.0 0.0 copy-start.1
  6.0 0.2 reshape.124
  6.2 0.4 copy.86
  6.6 46.6 %all_to_all.20 = bf16[64,2,2,2,512]{4,2,3,1,0:T(2,128)(2,1)S(1)} all-to-all(bf16[64,2,2,2,512]{4,2,3,1,0:T(2,128)(2,1)S(1)} %bitcast.83), channel_id=1, replica_groups=mesh['gx'=64,'gy'=8] {'gx'}, dimensions={0} | all-to-all | bytes 1048576 | tf_op jit(solution)/shard_map/all_to_all | solution.py:20
  53.2 0.2 convert_reduce_fusion
  53.4 23.8 %all_to_all.21 = f32[8,2,2,2,512]{4,3,2,1,0:T(2,128)S(1)} all-to-all(f32[8,2,2,2,512]{4,3,2,1,0:T(2,128)S(1)} %broadcast_in_dim.8), channel_id=1, replica_groups=mesh['gx'=64,'gy'=8] {'gy'}, dimensions={0} | all-to-all | bytes 262144 | tf_op jit(solution)/shard_map/all_to_all | solution.py:26
  77.3 0.0 copy-done.1
  77.3 0.1 fusion.26
  77.5 0.1 fusion.30
  77.6 0.1 fusion.18
  77.8 0.2 fusion.19
  78.0 0.1 reshape.133
  78.1 16.2 %all_to_all.22 = bf16[8,2,256]{2,1,0:T(2,128)(2,1)S(1)} all-to-all(bf16[8,2,256]{2,1,0:T(2,128)(2,1)S(1)} %reshape.133), channel_id=1, replica_groups=mesh['gx'=64,'gy'=8] {'gy'}, dimensions={0} | all-to-all | bytes 16384 | tf_op jit(solution)/shard_map/all_to_all | solution.py:26
  94.3 0.1 reshape.134
  94.4 0.1 reshape.132
  94.5 1.1 broadcast_in_dim.11
  95.5 10.2 %all-to-all-start.3 = ((bf16[64,2,2,2,512]{4,2,1,3,0:T(2,128)(2,1)}), bf16[64,2,2,2,512]{4,2,1,3,0:T(2,128)(2,1)}, u32[]{:S(2)}, u32[]{:S(2)}) async-start(bf16[64,2,2,2,512]{4,2,1,3,0:T(2,128)(2,1)} %broadcast_in_dim.11), calls=%async_computation.3 | async-start | bytes 1048576 | tf_op jit(solution)/shard_map/all_to_all | solution.py:26
  105.8 1.7 %fusion.23 = f32[2,512,512]{2,1,0:T(8,128)S(1)} fusion(bf16[2,512,512]{2,1,0:T(8,128)(2,1)S(1)} %bitcast.81, bf16[512,512]{1,0:T(8,128)(2,1)} %param.7), kind=kOutput, calls=%fused_computation.33 | convolution fusion | flops 536870912 | bytes 3670016 | tf_op jit(solution)/shard_map/bnc,cd->bnd/dot_general | solution.py:85
  107.5 27.8 %all-to-all-done.3 = bf16[64,2,2,2,512]{4,2,1,3,0:T(2,128)(2,1)} async-done(((bf16[64,2,2,2,512]{4,2,1,3,0:T(2,128)(2,1)}), bf16[64,2,2,2,512]{4,2,1,3,0:T(2,128)(2,1)}, u32[]{:S(2)}, u32[]{:S(2)}) %all-to-all-start.3) | async-done | bytes 524320 | tf_op jit(solution)/shard_map/all_to_all | solution.py:26
  135.3 2.2 %copy.76 = bf16[2,64,2,2,512]{4,2,1,0,3:T(2,128)(2,1)} copy(bf16[2,64,2,2,512]{4,2,0,3,1:T(2,128)(2,1)} %bitcast.13) | data formatting | bytes 1048576 | tf_op jit(solution)/shard_map/transpose | solution.py:38
  137.5 2.1 %reshape_reshape.3 = bf16[256,2,512]{2,0,1:T(8,128)(2,1)} reshape(bf16[2,64,2,2,512]{4,2,1,0,3:T(2,128)(2,1)} %copy.76) | data formatting | bytes 1048576 | tf_op jit(solution)/shard_map/reshape;reshape | solution.py:82
  139.5 3.0 %fusion.15 = bf16[2,512,512]{2,1,0:T(8,128)(2,1)} fusion(f32[2,512,512]{2,1,0:T(8,128)S(1)} %fusion.23, bf16[256,2,512]{2,0,1:T(8,128)(2,1)} %reshape_reshape.3, bf16[128,512]{0,1:T(8,128)(2,1)S(1)} %copy.64, bf16[128,512]{0,1:T(8,128)(2,1)S(1)} %copy.63), kind=kOutput, calls=%fused_computation.17 | convolution fusion | flops 274726912 | bytes 3932160 | tf_op jit(solution)/shard_map/kn,kbc->bnc/dot_general | solution.py:83
  142.5 5.5 %add_convert_fusion = bf16[2,512,512]{2,1,0:T(8,128)(2,1)} fusion(bf16[2,512,512]{2,1,0:T(8,128)(2,1)} %fusion.15, bf16[1024,512]{1,0:T(8,128)(2,1)} %param.9, bf16[1024,512]{1,0:T(8,128)(2,1)} %param.8), kind=kOutput, calls=%fused_computation.19 | convolution fusion | flops 2158493696 | bytes 4194304 | tf_op jit(solution)/shard_map/bnh,hc->bnc/dot_general | solution.py:93
  (13 shorter events, 0.2 us)
Async XLA Ops:
  0.0 5.6 %copy-start = (bf16[2,16,32,512]{3,2,1,0:T(8,128)(2,1)S(1)}, bf16[2,16,32,512]{3,2,1,0:T(8,128)(2,1)}, u32[]{:S(2)}) copy-start(bf16[2,16,32,512]{3,2,1,0:T(8,128)(2,1)} %param.5) | copy-start | bytes 3145732
  6.0 71.3 %copy-start.1 = (bf16[2,2,512,64]{2,3,1,0:T(8,128)(2,1)S(1)}, bf16[2,2,512,64]{2,3,1,0:T(8,128)(2,1)}, u32[]{:S(2)}) copy-start(bf16[2,2,512,64]{2,3,1,0:T(8,128)(2,1)} %param.6) | copy-start | bytes 786436
  95.5 39.7 %all-to-all-start.3 = ((bf16[64,2,2,2,512]{4,2,1,3,0:T(2,128)(2,1)}), bf16[64,2,2,2,512]{4,2,1,3,0:T(2,128)(2,1)}, u32[]{:S(2)}, u32[]{:S(2)}) async-start(bf16[64,2,2,2,512]{4,2,1,3,0:T(2,128)(2,1)} %broadcast_in_dim.11), calls=%async_computation.3 | async-start | bytes 1048576 | tf_op jit(solution)/shard_map/all_to_all | solution.py:26
where the time goes:
time: 149 us; the launch traced here: 148 us
  blocking collectives  86.6 us (58%)
  waiting for transfers between devices  27.8 us (19%)
  matrix products  11.3 us (8%)
  starting transfers between devices  10.2 us (7%)
  local copies, waits for them, and re-layouts  7.51 us (5%)
  other arithmetic  4.47 us (3%)
    all_to_all x1, blocking collectives, summed_on_arrival(): lax.all_to_all(cut_along(array, dim, count), axis, 0, 0, tiled=True)  46.6 us
    all_to_all x2, blocking collectives, copy_for_each(): lax.all_to_all(jnp.broadcast_to(array[None], (count, *array.shape)), axis...  40 us
    all_to_all x1, waiting for transfers between devices, copy_for_each(): lax.all_to_all(jnp.broadcast_to(array[None], (count, *array.shape)), axis...  27.8 us
    all_to_all x1, starting transfers between devices, copy_for_each(): lax.all_to_all(jnp.broadcast_to(array[None], (count, *array.shape)), axis...  10.2 us
    dot_general x1, matrix products, local(): jnp.einsum('bnh,hc->bnc', hidden, outer_weight, preferred_element_type=jn...  5.53 us
    another operation x1, other arithmetic  4.14 us
    dot_general x1, matrix products, local(): jnp.einsum('kn,kbc->bnc', basis, gathered, preferred_element_type=jnp.flo...  2.99 us
  transfers between devices with their start and end apart: 1, of which 1 were waited for; matrix products, arithmetic and copies ran while one was open for 1% of the time, Pallas kernels for 0%

commit v1 on v0

v1 whole, which is shorter than its diff:
```python
import math

import numpy as np
import jax
import jax.numpy as jnp
from jax import lax
from jax.experimental import pallas as pl
from jax.experimental.pallas import tpu as pltpu
from jax.sharding import PartitionSpec as P

MESH = pl.DeviceIdType.MESH
F32 = jnp.float32
BF16 = jnp.bfloat16
KX = 16
KY = 8
ROWS = 16
COLS = 32
CELLS = ROWS * COLS
NX = 1024
NY = 256
WIDTH = 512
HIDDEN = 1024
SPECTRUM_SCALE = 1.0 / math.sqrt(NX * NY)
FIELD_SCALE = 1.0 / math.sqrt(KX * KY)


def local_tables():
    core, y, j, z = np.meshgrid(np.arange(2), np.arange(4), np.arange(2), np.arange(8), indexing="ij")
    kx = (y * 4 + z // 2).reshape(2, 4, 16, 1, 1)
    ky = ((z % 2) * 4 + core * 2 + j).reshape(2, 4, 16, 1, 1)
    dx = np.arange(ROWS).reshape(1, 1, 1, ROWS, 1)
    dy = np.arange(COLS).reshape(1, 1, 1, 1, COLS)
    angle = 2.0 * np.pi * (kx * dx / NX + ky * dy / NY)
    angle = angle.reshape(2, 4, 16, CELLS)
    return np.stack([np.cos(angle), np.sin(angle)], axis=2).astype(np.float32)


def gelu(v):
    a = math.sqrt(2.0 / math.pi)
    t = jnp.tanh(v * (a + (a * 0.044715) * (v * v)))
    h = 0.5 * v
    return h + h * t


def body(
    field_hbm, weight_hbm, skip_hbm, inner_hbm, outer_hbm, table_hbm, out_ref,
    field, wv, skip, inner, outer, table,
    basis, basis_t, inner_t, pre,
    csend, crecv, own, xsend, xrecv, zsend, zrecv, ssend, srecv, gsend, grecv, blocks, spread,
    load_sem, cs_sem, cr_sem, xs_sem, xr_sem, zs_sem, zr_sem, ss_sem, sr_sem,
    gs_sem, gr_sem, bs_sem, br_sem, as_sem, ar_sem,
):
    gx, gy = lax.axis_index("gx"), lax.axis_index("gy")
    my, mzl, mc = gx // 16, (gx // 2) % 8, gx % 2
    mzh, mx = gy // 4, gy % 4
    mz = mzh * 8 + mzl

    def at(y, z, c, x):
        return (y * 16 + (z % 8) * 2 + c, (z // 8) * 4 + x)

    sibling = at(my, mz, 1 - mc, mx)
    plane = []
    for d in range(1, 16):
        x, y = (mx + d % 4) % 4, (my + d // 4) % 4
        plane.append((d, x, y, at(y, mz, mc, x)))
    column = []
    for d in (8, 7, 9, 6, 10, 5, 11, 4, 12, 3, 13, 2, 14, 1, 15):
        z = (mz + d) % 16
        column.append((d, z, at(my, z, mc, mx)))
    row = []
    for d in (2, 1, 3):
        x = (mx + d) % 4
        row.append((d, x, at(my, mz, mc, x)))

    barrier = pltpu.get_barrier_semaphore()
    for peer in [p[-1] for p in column] + [p[-1] for p in plane] + [sibling]:
        pl.semaphore_signal(barrier, inc=1, device_id=peer, device_id_type=MESH)

    loads = []

    def load(src, dst):
        copy = pltpu.make_async_copy(src, dst, load_sem.at[len(loads)])
        copy.start()
        loads.append(copy)
        return copy

    table_in = load(table_hbm, table)
    field_in = [load(field_hbm.at[b], field.at[b]) for b in range(2)]
    weight_in = [
        load(weight_hbm.at[j, q], wv.at[q, pl.ds(j * 64, 64)]) for j in range(2) for q in range(2)
    ]
    skip_in = load(skip_hbm, skip)
    inner_in = load(inner_hbm, inner)
    outer_in = load(outer_hbm, outer)

    index = lax.broadcasted_iota(jnp.int32, (16, 128), 0)
    table_in.wait()

    def make_basis(core):
        for y in range(4):
            j, z = index // 8, index % 8
            kx = y * 4 + z // 2
            ky = (z % 2) * 4 + core * 2 + j
            x_phase = ((kx * (gx * ROWS)) % NX).astype(F32) * (1.0 / NX)
            y_phase = ((ky * (gy * COLS)) % NY).astype(F32) * (1.0 / NY)
            phase = x_phase + y_phase
            phase = jnp.where(phase >= 1.0, phase - 1.0, phase)
            phase = jnp.where(phase >= 0.5, phase - 1.0, phase)
            c0 = jnp.cos(phase * (2.0 * math.pi))
            s0 = jnp.sin(phase * (2.0 * math.pi))
            for t in range(4):
                lanes = pl.ds(t * 128, 128)
                cd = table[core, y, 0, :, lanes]
                sd = table[core, y, 1, :, lanes]
                basis[core, y, 0, :, lanes] = (c0 * cd - s0 * sd).astype(BF16)
                basis[core, y, 1, :, lanes] = (-(s0 * cd + c0 * sd)).astype(BF16)

    def forward(core, b):
        rows = basis[core].reshape(128, CELLS)
        return jnp.dot(rows, field[b], preferred_element_type=F32)

    make_basis(1 - mc)
    core_copies = []
    for b in range(2):
        field_in[b].wait()
        part = forward(1 - mc, b)
        csend[b] = part.astype(BF16)
        if b == 0:
            pl.semaphore_wait(barrier, 31)
        copy = pltpu.make_async_remote_copy(
            src_ref=csend.at[b], dst_ref=crecv.at[b], send_sem=cs_sem.at[b], recv_sem=cr_sem.at[b],
            device_id=sibling, device_id_type=MESH,
        )
        copy.start()
        core_copies.append(copy)
    make_basis(mc)
    for b in range(2):
        own[b] = forward(mc, b)

    plane_copies = []
    for b in range(2):
        core_copies[b].wait_recv()
        for x in range(4):
            lanes = pl.ds(x * 128, 128)
            both = own[b, :, lanes] + crecv[b, :, lanes].astype(F32)
            own[b, :, lanes] = both
            xsend[b, x] = both.astype(BF16).reshape(4, 32, 128)
        for d, x, y, peer in plane:
            copy = pltpu.make_async_remote_copy(
                src_ref=xsend.at[b, x, y], dst_ref=xrecv.at[b, d], send_sem=xs_sem.at[b, d],
                recv_sem=xr_sem.at[b, d], device_id=peer, device_id_type=MESH,
            )
            copy.start()
            plane_copies.append(copy)

    skip_in.wait()
    for b in range(2):
        pre[b] = jnp.dot(field[b], skip[...], preferred_element_type=F32)

    for b in range(2):
        total = xsend[b, mx, my].astype(F32)
        for d in range(1, 16):
            plane_copies[b * 15 + d - 1].wait_recv()
            total = total + xrecv[b, d].astype(F32)
        for ri in range(2):
            for j in range(2):
                zsend[pl.ds(b * 4 + ri * 2 + j, 8, stride=8), :] = total[ri * 16 + j * 8 : ri * 16 + j * 8 + 8]

    column_copies = []
    for d, z, peer in column:
        copy = pltpu.make_async_remote_copy(
            src_ref=zsend.at[pl.ds(pl.multiple_of((z % 8) * 8, 8), 8)], dst_ref=zrecv.at[d],
            send_sem=zs_sem.at[d], recv_sem=zr_sem.at[d], device_id=peer, device_id_type=MESH,
        )
        copy.start()
        column_copies.append(copy)

    for core in range(2):
        for y in range(4):
            for ri in range(2):
                pass
    for t in range(4):
        cells = pl.ds(t * 128, 128)
        basis_t[cells, :] = basis[:, :, :, :, cells].reshape(256, 128).T
    inner_in.wait()
    for t in range(8):
        units = pl.ds(t * 128, 128)
        inner_t[:, units] = inner[units, :].T
    for copy in core_copies + plane_copies:
        copy.wait_send()

    total = zsend[pl.ds(pl.multiple_of(mzl * 8, 8), 8), :]
    for copy, (d, _, _) in zip(column_copies, column):
        copy.wait_recv()
        total = total + zrecv[d]
    spectrum = (total * SPECTRUM_SCALE).astype(BF16).astype(F32)

    ssend[...] = spectrum
    row_copies = []
    for d, x, peer in row:
        copy = pltpu.make_async_remote_copy(
            src_ref=ssend, dst_ref=srecv.at[mx], send_sem=ss_sem.at[d], recv_sem=sr_sem.at[d],
            device_id=peer, device_id_type=MESH,
        )
        copy.start()
        row_copies.append(copy)
    srecv[mx] = spectrum
    for copy in weight_in:
        copy.wait()
    for copy in column_copies:
        copy.wait_send()
    for copy in row_copies:
        copy.wait_recv()
    modes = jnp.concatenate([srecv[x] for x in range(4)], axis=1).astype(BF16)
    nt = (((1,), (1,)), ((), ()))
    by_re = lax.dot_general(modes, wv[0], nt, preferred_element_type=F32)
    by_im = lax.dot_general(modes, wv[1], nt, preferred_element_type=F32)
    low = lax.broadcasted_iota(jnp.int32, (1, 128), 1) < 64

    def pick(v, b, ri):
        k = b * 4 + ri * 2
        return jnp.where(low, v[k : k + 1], v[k + 1 : k + 2])

    mixed = []
    for b in range(2):
        mixed.append(pick(by_re, b, 0) - pick(by_im, b, 1))
        mixed.append(pick(by_im, b, 0) + pick(by_re, b, 1))
    mixed = jnp.concatenate(mixed + mixed, axis=0).astype(BF16).astype(F32)

    gsend[...] = mixed
    back_copies = []
    for d, z, peer in column:
        copy = pltpu.make_async_remote_copy(
            src_ref=gsend, dst_ref=grecv.at[pl.ds(pl.multiple_of(mz * 8, 8), 8)],
            send_sem=gs_sem.at[d], recv_sem=gr_sem.at[d], device_id=peer, device_id_type=MESH,
        )
        copy.start()
        back_copies.append(copy)
    grecv[pl.ds(pl.multiple_of(mz * 8, 8), 8), :] = mixed
    outer_in.wait()
    for copy in row_copies:
        copy.wait_send()
    for copy in back_copies:
        copy.wait_recv()

    low8 = lax.broadcasted_iota(jnp.int32, (8, 128), 1) < 64
    for b in range(2):
        for ri in range(2):
            k = b * 2 + ri
            first = grecv[pl.ds(k, 8, stride=8), :]
            second = grecv[pl.ds(64 + k, 8, stride=8), :]
            j0 = jnp.where(low8, first, pltpu.roll(second, 64, 1))
            j1 = jnp.where(low8, pltpu.roll(first, 64, 1), second)
            blocks[mx, my, b, ri] = jnp.concatenate([j0, j1], axis=0).astype(BF16)

    spread_copies = []
    for d, x, y, peer in plane:
        copy = pltpu.make_async_remote_copy(
            src_ref=blocks.at[mx, my], dst_ref=blocks.at[mx, my], send_sem=bs_sem.at[d],
            recv_sem=br_sem.at[d], device_id=peer, device_id_type=MESH,
        )
        copy.start()
        spread_copies.append(copy)
    for copy in back_copies:
        copy.wait_send()

    low16 = lax.broadcasted_iota(jnp.int32, (16, 128), 1) < 64
    pair_copies = []
    for dy in (0, 1, 3, 2):
        for dx in range(4):
            d = dy * 4 + dx
            if d:
                spread_copies[d - 1].wait_recv()
        y = (my + 4 - dy) % 4
        for b in range(2):
            for ri in range(2):
                for h in range(2):
                    even = blocks[2 * h, y, b, ri].astype(F32)
                    odd = blocks[2 * h + 1, y, b, ri].astype(F32)
                    near = jnp.where(low16, even, pltpu.roll(odd, 64, 1))
                    far = jnp.where(low16, pltpu.roll(even, 64, 1), odd)
                    spread[mc, y, b, ri, :, pl.ds(h * 128, 128)] = near.astype(BF16)
                    spread[mc, y, b, ri, :, pl.ds(256 + h * 128, 128)] = far.astype(BF16)
        copy = pltpu.make_async_remote_copy(
            src_ref=spread.at[mc, y], dst_ref=spread.at[mc, y], send_sem=as_sem.at[dy],
            recv_sem=ar_sem.at[dy], device_id=sibling, device_id_type=MESH,
        )
        copy.start()
        pair_copies.append(copy)
    for copy in spread_copies:
        copy.wait_send()
    for copy in pair_copies:
        copy.wait_recv()

    for b in range(2):
        modes = spread[:, :, b].reshape(256, WIDTH)
        for h in range(2):
            cells = pl.ds(h * 256, 256)
            spectral = jnp.dot(basis_t[cells, :], modes, preferred_element_type=F32)
            active = gelu(spectral * FIELD_SCALE + pre[b, cells, :]).astype(BF16)
            hidden = jnp.dot(active, inner_t[...], preferred_element_type=F32)
            hidden = gelu(hidden).astype(BF16)
            added = jnp.dot(hidden, outer[...], preferred_element_type=F32)
            out_ref[b, cells, :] = (active.astype(F32) + added).astype(BF16)
    for copy in pair_copies:
        copy.wait_send()


def local(grid_field, spectral_weight, skip_weight, inner_weight, outer_weight):
    table = jnp.asarray(local_tables())
    field = grid_field.reshape(2, CELLS, WIDTH)
    weight = jnp.swapaxes(spectral_weight, 2, 3)
    dma = pltpu.SemaphoreType.DMA
    out = pl.pallas_call(
        body,
        out_shape=jax.ShapeDtypeStruct((2, CELLS, WIDTH), BF16),
        in_specs=[pl.BlockSpec(memory_space=pl.ANY)] * 6,
        out_specs=pl.BlockSpec(memory_space=pltpu.VMEM),
        scratch_shapes=[
            pltpu.VMEM((2, CELLS, WIDTH), BF16),
            pltpu.VMEM((2, 128, WIDTH), BF16),
            pltpu.VMEM((WIDTH, WIDTH), BF16),
            pltpu.VMEM((HIDDEN, WIDTH), BF16),
            pltpu.VMEM((HIDDEN, WIDTH), BF16),
            pltpu.VMEM((2, 4, 2, 16, CELLS), F32),
            pltpu.VMEM((2, 4, 2, 16, CELLS), BF16),
            pltpu.VMEM((CELLS, 256), BF16),
            pltpu.VMEM((WIDTH, HIDDEN), BF16),
            pltpu.VMEM((2, CELLS, WIDTH), F32),
            pltpu.VMEM((2, 128, WIDTH), BF16),
            pltpu.VMEM((2, 128, WIDTH), BF16),
            pltpu.VMEM((2, 128, WIDTH), F32),
            pltpu.VMEM((2, 4, 4, 32, 128), BF16),
            pltpu.VMEM((2, 16, 32, 128), BF16),
            pltpu.VMEM((64, 128), F32),
            pltpu.VMEM((16, 8, 128), F32),
            pltpu.VMEM((8, 128), F32),
            pltpu.VMEM((4, 8, 128), F32),
            pltpu.VMEM((8, 128), F32),
            pltpu.VMEM((128, 128), F32),
            pltpu.VMEM((4, 4, 2, 2, 16, 128), BF16),
            pltpu.VMEM((2, 4, 2, 2, 16, WIDTH), BF16),
            dma((10,)),
            dma((2,)), dma((2,)),
            dma((2, 16)), dma((2, 16)),
            dma((16,)), dma((16,)),
            dma((4,)), dma((4,)),
            dma((16,)), dma((16,)),
            dma((16,)), dma((16,)),
            dma((4,)), dma((4,)),
        ],
        compiler_params=pltpu.CompilerParams(
            collective_id=0, has_side_effects=True, vmem_limit_bytes=40 << 20
        ),
        cost_estimate=pl.CostEstimate(flops=3_400_000_000, bytes_accessed=7 << 20, transcendentals=1_600_000),
    )(field, weight, skip_weight, inner_weight, outer_weight, table)
    return out.reshape(grid_field.shape)


def solution(mesh):
    in_specs = (P(None, "gx", "gy", None), P("gx", None, None, "gy"), P(), P(), P())
    out_specs = P(None, "gx", "gy", None)
    return jax.shard_map(local, mesh=mesh, in_specs=in_specs, out_specs=out_specs, check_vma=False)
```

time: 149 us -> 64.4 us (0.43)
  blocking collectives: 86.6 us -> 0 us
  Pallas kernels: 0 us -> 56.3 us
  waiting for transfers between devices: 27.8 us -> 0 us
  matrix products: 11.3 us -> 0 us
  starting transfers between devices: 10.2 us -> 0 us
  other arithmetic: 4.47 us -> 0 us
    all_to_all x3 -> x0, blocking collectives: 86.6 us -> none  [the longest x1 46.6 us: summed_on_arrival(): lax.all_to_all(cut_along(array, dim, count), axis, 0, 0, tiled=True)]
    pallas_call x0 -> x1, Pallas kernels: none -> 56.3 us  [local(): pl.pallas_call(body, out_shape=jax.ShapeDtypeStruct((2, CELLS, WIDTH), BF...]
    all_to_all x1 -> x0, waiting for transfers between devices: 27.8 us -> none  [copy_for_each(): lax.all_to_all(jnp.broadcast_to(array[None], (count, *array.shape)), axis...]
    dot_general x8 -> x0, matrix products: 11.3 us -> none  [the longest x1 5.53 us: local(): jnp.einsum('bnh,hc->bnc', hidden, outer_weight, preferred_element_type=jn...]
    all_to_all x1 -> x0, starting transfers between devices: 10.2 us -> none  [copy_for_each(): lax.all_to_all(jnp.broadcast_to(array[None], (count, *array.shape)), axis...]
    unnamed x7 -> x13, local copies, waits for them, and re-layouts: 0.2 us -> 7.68 us
    another operation x2 -> x0, other arithmetic: 4.16 us -> none
    transpose x2 -> x0, local copies, waits for them, and re-layouts: 2.21 us -> none  [laid_out(): return jnp.moveaxis(blocks, 0, dim).reshape(dims)]
  transfers between devices with their start and end apart: 1 -> 0, of which waited for: 1 -> 0; matrix products, arithmetic and copies ran while one was open for 1% -> 0% of each run, Pallas kernels for 0% -> 0%
where the time goes in v1:
time: 64.4 us; the launch traced here: 64 us
  Pallas kernels  56.3 us (87%)
  local copies, waits for them, and re-layouts  7.68 us (12%)
    pallas_call x1, Pallas kernels, local(): pl.pallas_call(body, out_shape=jax.ShapeDtypeStruct((2, CELLS, WIDTH), BF...  56.3 us
    unnamed x13, local copies, waits for them, and re-layouts  7.68 us

profile of v1, /device:TPU:1, one launch (start us, length us, event | category | flops | bytes accessed | tf_op | source)
XLA Modules:
  0.0 64.0 jit_solution(10458828709280609264)
XLA Ops:
  0.0 0.0 copy-start
  0.0 1.2 %copy-done = bf16[2,16,32,512]{3,2,1,0:T(8,128)(2,1)S(1)} copy-done((bf16[2,16,32,512]{3,2,1,0:T(8,128)(2,1)S(1)}, bf16[2,16,32,512]{3,2,1,0:T(8,128)(2,1)}, u32[]{:S(2)}) %copy-start) | copy-done | bytes 1048600
  1.2 0.0 copy-start.1
  1.2 1.2 %copy-done.1 = bf16[1024,512]{1,0:T(8,128)(2,1)S(1)} copy-done((bf16[1024,512]{1,0:T(8,128)(2,1)S(1)}, bf16[1024,512]{1,0:T(8,128)(2,1)}, u32[]{:S(2)}) %copy-start.1) | copy-done | bytes 1048600
  2.5 0.0 copy-start.2
  2.5 1.2 %copy-done.2 = bf16[1024,512]{1,0:T(8,128)(2,1)S(1)} copy-done((bf16[1024,512]{1,0:T(8,128)(2,1)S(1)}, bf16[1024,512]{1,0:T(8,128)(2,1)}, u32[]{:S(2)}) %copy-start.2) | copy-done | bytes 1048600
  3.7 0.0 copy-start.3
  3.7 1.0 %copy-done.3 = bf16[512,512]{1,0:T(8,128)(2,1)S(1)} copy-done((bf16[512,512]{1,0:T(8,128)(2,1)S(1)}, bf16[512,512]{1,0:T(8,128)(2,1)}, u32[]{:S(2)}) %copy-start.3) | copy-done | bytes 524312
  4.7 0.0 copy-start.4
  4.7 0.9 %copy-done.4 = bf16[2,2,512,64]{2,3,1,0:T(8,128)(2,1)S(1)} copy-done((bf16[2,2,512,64]{2,3,1,0:T(8,128)(2,1)S(1)}, bf16[2,2,512,64]{2,3,1,0:T(8,128)(2,1)}, u32[]{:S(2)}) %copy-start.4) | copy-done | bytes 262168
  5.7 0.0 copy-start.5
  5.7 1.0 %copy-done.5 = f32[2,4,2,16,512]{4,3,2,1,0:T(8,128)S(1)} copy-done((f32[2,4,2,16,512]{4,3,2,1,0:T(8,128)S(1)}, f32[2,4,2,16,512]{4,3,2,1,0:T(8,128)}, u32[]{:S(2)}) %copy-start.5) | copy-done | bytes 524312
  6.7 56.3 %shard_map.64 = bf16[2,512,512]{2,1,0:T(8,128)(2,1)S(1)} custom-call(bf16[2,512,512]{2,1,0:T(8,128)(2,1)S(1)} %bitcast.4, bf16[2,2,64,512]{3,2,1,0:T(8,128)(2,1)S(1)} %bitcast.5, bf16[512,512]{1,0:T(8,128)(2,1)S(1)} %copy-done.3, bf16[1024,512]{1,0:T(8,128)(2,1)S(1)} %copy-done.1, bf16[1024,512]{1,0:T(8,128)(2,1)S(1)} %copy-done.2, ...), custom_call_target="tpu_custom_call" | custom-call | flops 3400000000 | bytes 7340032 | tf_op jit(solution)/shard_map/pallas_call | solution.py:314
  63.1 1.0 %copy.8 = bf16[2,16,32,512]{3,2,1,0:T(8,128)(2,1)} copy(bf16[2,16,32,512]{3,2,1,0:T(8,128)(2,1)S(1)} %bitcast.3) | data formatting | bytes 2097152
Async XLA Ops:
  0.0 1.2 %copy-start = (bf16[2,16,32,512]{3,2,1,0:T(8,128)(2,1)S(1)}, bf16[2,16,32,512]{3,2,1,0:T(8,128)(2,1)}, u32[]{:S(2)}) copy-start(bf16[2,16,32,512]{3,2,1,0:T(8,128)(2,1)} %param.6) | copy-start | bytes 3145732
  1.2 1.2 %copy-start.1 = (bf16[1024,512]{1,0:T(8,128)(2,1)S(1)}, bf16[1024,512]{1,0:T(8,128)(2,1)}, u32[]{:S(2)}) copy-start(bf16[1024,512]{1,0:T(8,128)(2,1)} %inner_hbm.1) | copy-start | bytes 3145732
  2.5 1.2 %copy-start.2 = (bf16[1024,512]{1,0:T(8,128)(2,1)S(1)}, bf16[1024,512]{1,0:T(8,128)(2,1)}, u32[]{:S(2)}) copy-start(bf16[1024,512]{1,0:T(8,128)(2,1)} %outer_hbm.1) | copy-start | bytes 3145732
  3.7 1.0 %copy-start.3 = (bf16[512,512]{1,0:T(8,128)(2,1)S(1)}, bf16[512,512]{1,0:T(8,128)(2,1)}, u32[]{:S(2)}) copy-start(bf16[512,512]{1,0:T(8,128)(2,1)} %skip_hbm.1) | copy-start | bytes 1572868
  4.7 0.9 %copy-start.4 = (bf16[2,2,512,64]{2,3,1,0:T(8,128)(2,1)S(1)}, bf16[2,2,512,64]{2,3,1,0:T(8,128)(2,1)}, u32[]{:S(2)}) copy-start(bf16[2,2,512,64]{2,3,1,0:T(8,128)(2,1)} %param.7) | copy-start | bytes 786436
  5.7 1.0 %copy-start.5 = (f32[2,4,2,16,512]{4,3,2,1,0:T(8,128)S(1)}, f32[2,4,2,16,512]{4,3,2,1,0:T(8,128)}, u32[]{:S(2)}) copy-start(f32[2,4,2,16,512]{4,3,2,1,0:T(8,128)} %constant.2.clone.table_hbm) | copy-start | bytes 1572868

commit v2 on v1

--- a/solution.py
+++ b/solution.py
@@ -43,12 +43,12 @@
 
 
 def body(
-    field_hbm, weight_hbm, skip_hbm, inner_hbm, outer_hbm, table_hbm, out_ref,
+    field_hbm, weight_hbm, skip_hbm, inner_hbm, outer_hbm, table_hbm, out_hbm,
     field, wv, skip, inner, outer, table,
     basis, basis_t, inner_t, pre,
-    csend, crecv, own, xsend, xrecv, zsend, zrecv, ssend, srecv, gsend, grecv, blocks, spread,
+    csend, crecv, own, xsend, xrecv, zsend, zrecv, ssend, srecv, gsend, grecv, blocks, spread, result,
     load_sem, cs_sem, cr_sem, xs_sem, xr_sem, zs_sem, zr_sem, ss_sem, sr_sem,
-    gs_sem, gr_sem, bs_sem, br_sem, as_sem, ar_sem,
+    gs_sem, gr_sem, bs_sem, br_sem, as_sem, ar_sem, store_sem, across_ready, near_ready, far_ready,
 ):
     gx, gy = lax.axis_index("gx"), lax.axis_index("gy")
     my, mzl, mc = gx // 16, (gx // 2) % 8, gx % 2
@@ -72,9 +72,15 @@
         x = (mx + d) % 4
         row.append((d, x, at(my, mz, mc, x)))
 
+    def signal(semaphore, peers):
+        for peer in peers:
+            pl.semaphore_signal(semaphore, inc=1, device_id=peer, device_id_type=MESH)
+
     barrier = pltpu.get_barrier_semaphore()
-    for peer in [p[-1] for p in column] + [p[-1] for p in plane] + [sibling]:
-        pl.semaphore_signal(barrier, inc=1, device_id=peer, device_id_type=MESH)
+    across = [at((my + d) % 4, mz, mc, mx) for d in (2, 1, 3)]
+    along = {d: at(my, (mz + d) % 16, mc, mx) for d in (1, 2, 4, 12, 14, 15)}
+    near = [sibling] + [p[-1] for p in row] + across + [along[d] for d in (2, 14, 1, 15)]
+    signal(barrier, near)
 
     loads = []
 
@@ -84,56 +90,63 @@
         loads.append(copy)
         return copy
 
-    table_in = load(table_hbm, table)
+    first_in = load(table_hbm.at[1 - mc], table.at[1 - mc])
     field_in = [load(field_hbm.at[b], field.at[b]) for b in range(2)]
+    second_in = load(table_hbm.at[mc], table.at[mc])
+
+    index = lax.broadcasted_iota(jnp.int32, (16, 128), 0)
+    lane = lax.broadcasted_iota(jnp.int32, (16, 128), 1)
+    kx = (lane % 4) * 4 + (index % 8) // 2
+    ky = (index % 2) * 4 + jnp.where(lane < 4, 1 - mc, mc) * 2 + index // 8
+    x_phase = ((kx * (gx * ROWS)) % NX).astype(F32) * (1.0 / NX)
+    y_phase = ((ky * (gy * COLS)) % NY).astype(F32) * (1.0 / NY)
+    phase = x_phase + y_phase
+    phase = jnp.where(phase >= 1.0, phase - 1.0, phase)
+    phase = jnp.where(phase >= 0.5, phase - 1.0, phase)
+    cos0 = jnp.cos(phase * (2.0 * math.pi))
+    sin0 = jnp.sin(phase * (2.0 * math.pi))
+
+    def make_basis(core, column0):
+        for y in range(4):
+            at_lane = slice(column0 + y, column0 + y + 1)
+            c0 = jnp.broadcast_to(cos0[:, at_lane], (16, 128))
+            s0 = jnp.broadcast_to(sin0[:, at_lane], (16, 128))
+            for t in range(4):
+                lanes = pl.ds(t * 128, 128)
+                cd = table[core, y, 0, :, lanes]
+                sd = table[core, y, 1, :, lanes]
+                basis[core, y, 0, :, lanes] = (c0 * cd - s0 * sd).astype(BF16)
+                basis[core, y, 1, :, lanes] = (-(s0 * cd + c0 * sd)).astype(BF16)
+
+    def forward(core, b):
+        rows = basis[core].reshape(128, CELLS)
+        return jnp.dot(rows, field[b], preferred_element_type=F32)
+
+    first_in.wait()
+    make_basis(1 - mc, 0)
+    core_copies = []
+    for b in range(2):
+        field_in[b].wait()
+        part = forward(1 - mc, b)
+        csend[b] = part.astype(BF16)
+        if b == 0:
+            pl.semaphore_wait(barrier, 11)
+            signal(across_ready, across)
+            signal(near_ready, [along[2], along[14]])
+        copy = pltpu.make_async_remote_copy(
+            src_ref=csend.at[b], dst_ref=crecv.at[b], send_sem=cs_sem.at[b], recv_sem=cr_sem.at[b],
+            device_id=sibling, device_id_type=MESH,
+        )
+        copy.start()
+        core_copies.append(copy)
     weight_in = [
         load(weight_hbm.at[j, q], wv.at[q, pl.ds(j * 64, 64)]) for j in range(2) for q in range(2)
     ]
     skip_in = load(skip_hbm, skip)
     inner_in = load(inner_hbm, inner)
     outer_in = load(outer_hbm, outer)
-
-    index = lax.broadcasted_iota(jnp.int32, (16, 128), 0)
-    table_in.wait()
-
-    def make_basis(core):
-        for y in range(4):
-            j, z = index // 8, index % 8
-            kx = y * 4 + z // 2
-            ky = (z % 2) * 4 + core * 2 + j
-            x_phase = ((kx * (gx * ROWS)) % NX).astype(F32) * (1.0 / NX)
-            y_phase = ((ky * (gy * COLS)) % NY).astype(F32) * (1.0 / NY)
-            phase = x_phase + y_phase
-            phase = jnp.where(phase >= 1.0, phase - 1.0, phase)
-            phase = jnp.where(phase >= 0.5, phase - 1.0, phase)
-            c0 = jnp.cos(phase * (2.0 * math.pi))
-            s0 = jnp.sin(phase * (2.0 * math.pi))
-            for t in range(4):
-                lanes = pl.ds(t * 128, 128)
-                cd = table[core, y, 0, :, lanes]
-                sd = table[core, y, 1, :, lanes]
-                basis[core, y, 0, :, lanes] = (c0 * cd - s0 * sd).astype(BF16)
-                basis[core, y, 1, :, lanes] = (-(s0 * cd + c0 * sd)).astype(BF16)
-
-    def forward(core, b):
-        rows = basis[core].reshape(128, CELLS)
-        return jnp.dot(rows, field[b], preferred_element_type=F32)
-
-    make_basis(1 - mc)
-    core_copies = []
-    for b in range(2):
-        field_in[b].wait()
-        part = forward(1 - mc, b)
-        csend[b] = part.astype(BF16)
-        if b == 0:
-            pl.semaphore_wait(barrier, 31)
-        copy = pltpu.make_async_remote_copy(
-            src_ref=csend.at[b], dst_ref=crecv.at[b], send_sem=cs_sem.at[b], recv_sem=cr_sem.at[b],
-            device_id=sibling, device_id_type=MESH,
-        )
-        copy.start()
-        core_copies.append(copy)
-    make_basis(mc)
+    second_in.wait()
+    make_basis(mc, 4)
     for b in range(2):
         own[b] = forward(mc, b)
 
@@ -145,6 +158,8 @@
             both = own[b, :, lanes] + crecv[b, :, lanes].astype(F32)
             own[b, :, lanes] = both
             xsend[b, x] = both.astype(BF16).reshape(4, 32, 128)
+        if b == 0:
+            pl.semaphore_wait(across_ready, 3)
         for d, x, y, peer in plane:
             copy = pltpu.make_async_remote_copy(
                 src_ref=xsend.at[b, x, y], dst_ref=xrecv.at[b, d], send_sem=xs_sem.at[b, d],
@@ -153,6 +168,8 @@
             copy.start()
             plane_copies.append(copy)
 
+    pl.semaphore_wait(near_ready, 2)
+    signal(far_ready, [along[4], along[12]])
     skip_in.wait()
     for b in range(2):
         pre[b] = jnp.dot(field[b], skip[...], preferred_element_type=F32)
@@ -166,6 +183,7 @@
             for j in range(2):
                 zsend[pl.ds(b * 4 + ri * 2 + j, 8, stride=8), :] = total[ri * 16 + j * 8 : ri * 16 + j * 8 + 8]
 
+    pl.semaphore_wait(far_ready, 2)
     column_copies = []
     for d, z, peer in column:
         copy = pltpu.make_async_remote_copy(
@@ -175,10 +193,6 @@
         copy.start()
         column_copies.append(copy)
 
-    for core in range(2):
-        for y in range(4):
-            for ri in range(2):
-                pass
     for t in range(4):
         cells = pl.ds(t * 128, 128)
         basis_t[cells, :] = basis[:, :, :, :, cells].reshape(256, 128).T
@@ -292,6 +306,7 @@
     for copy in pair_copies:
         copy.wait_recv()
 
+    stores = []
     for b in range(2):
         modes = spread[:, :, b].reshape(256, WIDTH)
         for h in range(2):
@@ -301,9 +316,16 @@
             hidden = jnp.dot(active, inner_t[...], preferred_element_type=F32)
             hidden = gelu(hidden).astype(BF16)
             added = jnp.dot(hidden, outer[...], preferred_element_type=F32)
-            out_ref[b, cells, :] = (active.astype(F32) + added).astype(BF16)
+            result[b, cells, :] = (active.astype(F32) + added).astype(BF16)
+            copy = pltpu.make_async_copy(
+                result.at[b, cells], out_hbm.at[b, cells], store_sem.at[b * 2 + h]
+            )
+            copy.start()
+            stores.append(copy)
     for copy in pair_copies:
         copy.wait_send()
+    for copy in stores:
+        copy.wait()
 
 
 def local(grid_field, spectral_weight, skip_weight, inner_weight, outer_weight):
@@ -314,8 +336,8 @@
     out = pl.pallas_call(
         body,
         out_shape=jax.ShapeDtypeStruct((2, CELLS, WIDTH), BF16),
-        in_specs=[pl.BlockSpec(memory_space=pl.ANY)] * 6,
-        out_specs=pl.BlockSpec(memory_space=pltpu.VMEM),
+        in_specs=[pl.BlockSpec(memory_space=pltpu.HBM)] * 6,
+        out_specs=pl.BlockSpec(memory_space=pltpu.HBM),
         scratch_shapes=[
             pltpu.VMEM((2, CELLS, WIDTH), BF16),
             pltpu.VMEM((2, 128, WIDTH), BF16),
@@ -340,7 +362,8 @@
             pltpu.VMEM((128, 128), F32),
             pltpu.VMEM((4, 4, 2, 2, 16, 128), BF16),
             pltpu.VMEM((2, 4, 2, 2, 16, WIDTH), BF16),
-            dma((10,)),
+            pltpu.VMEM((2, CELLS, WIDTH), BF16),
+            dma((12,)),
             dma((2,)), dma((2,)),
             dma((2, 16)), dma((2, 16)),
             dma((16,)), dma((16,)),
@@ -348,9 +371,11 @@
             dma((16,)), dma((16,)),
             dma((16,)), dma((16,)),
             dma((4,)), dma((4,)),
+            dma((4,)),
+            pltpu.SemaphoreType.REGULAR, pltpu.SemaphoreType.REGULAR, pltpu.SemaphoreType.REGULAR,
         ],
         compiler_params=pltpu.CompilerParams(
-            collective_id=0, has_side_effects=True, vmem_limit_bytes=40 << 20
+            collective_id=0, has_side_effects=True, vmem_limit_bytes=63_000_000
         ),
         cost_estimate=pl.CostEstimate(flops=3_400_000_000, bytes_accessed=7 << 20, transcendentals=1_600_000),
     )(field, weight, skip_weight, inner_weight, outer_weight, table)

time: 64.4 us -> 55.4 us (0.86)
  local copies, waits for them, and re-layouts: 7.68 us -> 2.3 us
  Pallas kernels: 56.3 us -> 52.9 us
    unnamed x13 -> x1, local copies, waits for them, and re-layouts: 7.68 us -> 2.3 us
    pallas_call x1, Pallas kernels: 56.3 us -> 52.9 us  [local(): pl.pallas_call(body, out_shape=jax.ShapeDtypeStruct((2, CELLS, WIDTH), BF...]
where the time goes in v2:
time: 55.4 us; the launch traced here: 55.2 us
  Pallas kernels  52.9 us (95%)
  local copies, waits for them, and re-layouts  2.3 us (4%)
    pallas_call x1, Pallas kernels, local(): pl.pallas_call(body, out_shape=jax.ShapeDtypeStruct((2, CELLS, WIDTH), BF...  52.9 us
    unnamed x1, local copies, waits for them, and re-layouts  2.3 us

profile of v2, /device:TPU:1, one launch (start us, length us, event | category | flops | bytes accessed | tf_op | source)
XLA Modules:
  0.0 55.2 jit_solution(14248524574648347750)
XLA Ops:
  0.0 52.9 %shard_map.64 = bf16[2,512,512]{2,1,0:T(8,128)(2,1)} custom-call(bf16[2,512,512]{2,1,0:T(8,128)(2,1)} %bitcast.4, bf16[2,2,64,512]{3,2,1,0:T(8,128)(2,1)} %bitcast.5, bf16[512,512]{1,0:T(8,128)(2,1)} %skip_hbm.1, bf16[1024,512]{1,0:T(8,128)(2,1)} %inner_hbm.1, bf16[1024,512]{1,0:T(8,128)(2,1)} %outer_hbm.1, f32[2,4,2,16,512]{4,3,2,1,0:T(8,128)} %constant.2.clone.table_hbm), custom_call_target="tpu_custom_call" | custom-call | flops 3400000000 | bytes 7340032 | tf_op jit(solution)/shard_map/pallas_call | solution.py:336
  52.9 2.3 %copy.8 = bf16[2,16,32,512]{3,2,1,0:T(8,128)(2,1)} copy(bf16[2,16,32,512]{3,2,1,0:T(8,128)(2,1)} %bitcast.3) | data formatting | bytes 2097152

commit v3 on v2

v3 whole, which is shorter than its diff:
```python
import math

import numpy as np
import jax
import jax.numpy as jnp
from jax import lax
from jax.experimental import pallas as pl
from jax.experimental.pallas import tpu as pltpu
from jax.sharding import PartitionSpec as P

MESH = pl.DeviceIdType.MESH
F32 = jnp.float32
BF16 = jnp.bfloat16
KX = 16
KY = 8
ROWS = 16
COLS = 32
CELLS = ROWS * COLS
NX = 1024
NY = 256
WIDTH = 512
HIDDEN = 1024
SPECTRUM_SCALE = 1.0 / math.sqrt(NX * NY)
FIELD_SCALE = 1.0 / math.sqrt(KX * KY)


def local_tables():
    core, y, j, z = np.meshgrid(np.arange(2), np.arange(4), np.arange(2), np.arange(8), indexing="ij")
    kx = (y * 4 + z // 2).reshape(2, 4, 16, 1, 1)
    ky = ((z % 2) * 4 + core * 2 + j).reshape(2, 4, 16, 1, 1)
    dx = np.arange(ROWS).reshape(1, 1, 1, ROWS, 1)
    dy = np.arange(COLS).reshape(1, 1, 1, 1, COLS)
    angle = 2.0 * np.pi * (kx * dx / NX + ky * dy / NY)
    angle = angle.reshape(2, 4, 16, CELLS)
    return np.stack([np.cos(angle), np.sin(angle)], axis=2).astype(np.float32)


def gelu(v):
    a = math.sqrt(2.0 / math.pi)
    t = jnp.tanh(v * (a + (a * 0.044715) * (v * v)))
    h = 0.5 * v
    return h + h * t


def body(
    field_hbm, weight_hbm, skip_hbm, inner_hbm, outer_hbm, table_hbm, out_ref,
    field, wv, skip, inner, outer, table,
    basis, basis_t, inner_t, pre,
    csend, crecv, own, xsend, xrecv, zsend, zrecv, gsend, grecv, held, spread,
    load_sem, cs_sem, cr_sem, xs_sem, xr_sem, zs_sem, zr_sem, ss_sem, sr_sem,
    gs_sem, gr_sem, bs_sem, br_sem, as_sem, ar_sem, across_ready, near_ready, far_ready,
):
    gx, gy = lax.axis_index("gx"), lax.axis_index("gy")
    my, mzl, mc = gx // 16, (gx // 2) % 8, gx % 2
    mzh, mx = gy // 4, gy % 4
    mz = mzh * 8 + mzl

    def at(y, z, c, x):
        return (y * 16 + (z % 8) * 2 + c, (z // 8) * 4 + x)

    sibling = at(my, mz, 1 - mc, mx)
    def partner(x, y):
        return at(y % 4, mz, mc, x % 4)

    steps = (10, 6, 14, 9, 11, 5, 7, 13, 15, 2, 8, 1, 3, 4, 12)
    batch, half = mx // 2, mx % 2
    column = []
    for d in (8, 7, 9, 6, 10, 5, 11, 4, 12, 3, 13, 2, 14, 1, 15):
        z = (mz + d) % 16
        column.append((d, z, at(my, z, mc, mx)))
    row = []
    for d in (2, 1, 3):
        x = (mx + d) % 4
        row.append((d, x, at(my, mz, mc, x)))

    def signal(semaphore, peers):
        for peer in peers:
            pl.semaphore_signal(semaphore, inc=1, device_id=peer, device_id_type=MESH)

    barrier = pltpu.get_barrier_semaphore()
    across = [at((my + d) % 4, mz, mc, mx) for d in (2, 1, 3)]
    along = {d: at(my, (mz + d) % 16, mc, mx) for d in (1, 2, 4, 12, 14, 15)}
    near = [sibling] + [p[-1] for p in row] + across + [along[d] for d in (2, 14, 1, 15)]
    signal(barrier, near)

    loads = []

    def load(src, dst):
        copy = pltpu.make_async_copy(src, dst, load_sem.at[len(loads)])
        copy.start()
        loads.append(copy)
        return copy

    first_in = load(table_hbm.at[1 - mc], table.at[1 - mc])
    field_in = [load(field_hbm.at[b], field.at[b]) for b in range(2)]
    second_in = load(table_hbm.at[mc], table.at[mc])

    index = lax.broadcasted_iota(jnp.int32, (16, 128), 0)
    lane = lax.broadcasted_iota(jnp.int32, (16, 128), 1)
    kx = (lane % 4) * 4 + (index % 8) // 2
    ky = (index % 2) * 4 + jnp.where(lane < 4, 1 - mc, mc) * 2 + index // 8
    x_phase = ((kx * (gx * ROWS)) % NX).astype(F32) * (1.0 / NX)
    y_phase = ((ky * (gy * COLS)) % NY).astype(F32) * (1.0 / NY)
    phase = x_phase + y_phase
    phase = jnp.where(phase >= 1.0, phase - 1.0, phase)
    phase = jnp.where(phase >= 0.5, phase - 1.0, phase)
    cos0 = jnp.cos(phase * (2.0 * math.pi))
    sin0 = jnp.sin(phase * (2.0 * math.pi))

    def make_basis(core, column0):
        for y in range(4):
            at_lane = slice(column0 + y, column0 + y + 1)
            c0 = jnp.broadcast_to(cos0[:, at_lane], (16, 128))
            s0 = jnp.broadcast_to(sin0[:, at_lane], (16, 128))
            for t in range(4):
                lanes = pl.ds(t * 128, 128)
                cd = table[core, y, 0, :, lanes]
                sd = table[core, y, 1, :, lanes]
                re = c0 * cd - s0 * sd
                im = -(s0 * cd + c0 * sd)
                for j in range(2):
                    rows = slice(j * 8, j * 8 + 8)
                    both = jnp.concatenate([re[rows], im[rows]], axis=0)
                    basis[core, y, j, :, lanes] = both.astype(BF16)

    def forward(core, b):
        rows = basis[core].reshape(128, CELLS)
        return jnp.dot(rows, field[b], preferred_element_type=F32)

    first_in.wait()
    make_basis(1 - mc, 0)
    core_copies = []
    for b in range(2):
        field_in[b].wait()
        part = forward(1 - mc, b)
        csend[b] = part.astype(BF16)
        if b == 0:
            pl.semaphore_wait(barrier, 11)
            signal(across_ready, across)
            signal(near_ready, [along[2], along[14]])
        copy = pltpu.make_async_remote_copy(
            src_ref=csend.at[b], dst_ref=crecv.at[b], send_sem=cs_sem.at[b], recv_sem=cr_sem.at[b],
            device_id=sibling, device_id_type=MESH,
        )
        copy.start()
        core_copies.append(copy)
    weight_in = load(weight_hbm.at[half], wv.at[:, pl.ds(pl.multiple_of(mx * 64, 64), 64)])
    skip_in = load(skip_hbm, skip)
    inner_in = load(inner_hbm, inner)
    outer_in = load(outer_hbm, outer)
    second_in.wait()
    make_basis(mc, 4)
    for b in range(2):
        own[b] = forward(mc, b)

    def plane_copy(x, dx, y, dy):
        return pltpu.make_async_remote_copy(
            src_ref=xsend.at[x // 2, (y % 4) * 2 + x % 2], dst_ref=xrecv.at[dy * 4 + dx],
            send_sem=xs_sem.at[dy * 4 + dx], recv_sem=xr_sem.at[dy * 4 + dx],
            device_id=partner(x, y), device_id_type=MESH,
        )

    for b in range(2):
        core_copies[b].wait_recv()
        xsend[b] = (own[b] + crecv[b].astype(F32)).astype(BF16).reshape(8, 16, WIDTH)
        if b == 0:
            pl.semaphore_wait(across_ready, 3)
        for dy in (2, 1, 3, 0):
            for x in (2 * b, 2 * b + 1):
                dx = (x + 4 - mx) % 4
                if dy:
                    plane_copy(x, dx, my + dy, dy).start()
                else:

                    @pl.when(dx != 0)
                    def _():
                        plane_copy(x, dx, my, 0).start()

    pl.semaphore_wait(near_ready, 2)
    signal(far_ready, [along[4], along[12]])
    skip_in.wait()
    for b in range(2):
        pre[b] = jnp.dot(field[b], skip[...], preferred_element_type=F32)

    row_copies = []
    for d, x, peer in row:
        copy = pltpu.make_async_remote_copy(
            src_ref=weight_hbm.at[x % 2], dst_ref=wv.at[:, pl.ds(pl.multiple_of(mx * 64, 64), 64)],
            send_sem=ss_sem.at[d], recv_sem=sr_sem.at[d], device_id=peer, device_id_type=MESH,
        )
        copy.start()
        row_copies.append(copy)

    mine = pl.ds(pl.multiple_of((my * 2 + half) * 16, 16), 16)
    total = own[batch, mine, :] + crecv[batch, mine, :].astype(F32)
    plane_copies = [plane_copy((mx + d) % 4, d % 4, my + d // 4, d // 4) for d in steps]
    for copy, d in reversed(list(zip(plane_copies, steps))):
        copy.wait_recv()
        total = total + xrecv[d].astype(F32)
    for ri in range(2):
        for t in range(4):
            zsend[pl.ds(ri * 4 + t, 8, stride=8), :] = total[ri * 8 : ri * 8 + 8, t * 128 : t * 128 + 128]

    pl.semaphore_wait(far_ready, 2)
    column_copies = []
    for d, z, peer in column:
        copy = pltpu.make_async_remote_copy(
            src_ref=zsend.at[pl.ds(pl.multiple_of((z % 8) * 8, 8), 8)], dst_ref=zrecv.at[d],
            send_sem=zs_sem.at[d], recv_sem=zr_sem.at[d], device_id=peer, device_id_type=MESH,
        )
        copy.start()
        column_copies.append(copy)

    for t in range(4):
        cells = pl.ds(t * 128, 128)
        basis_t[cells, :] = basis[:, :, :, :, cells].reshape(256, 128).T
    inner_in.wait()
    for t in range(8):
        units = pl.ds(t * 128, 128)
        inner_t[:, units] = inner[units, :].T
    for copy in core_copies + plane_copies:
        copy.wait_send()

    total = zsend[pl.ds(pl.multiple_of(mzl * 8, 8), 8), :]
    for copy, (d, _, _) in reversed(list(zip(column_copies, column))):
        copy.wait_recv()
        total = total + zrecv[d]
    spectrum = (total * SPECTRUM_SCALE).astype(BF16).astype(F32)

    weight_in.wait()
    for copy in row_copies:
        copy.wait_recv()
    parts = [
        jnp.concatenate([spectrum[ri * 4 + t : ri * 4 + t + 1] for t in range(4)], axis=1)
        for ri in range(2)
    ]
    modes = jnp.concatenate(parts * 4, axis=0).astype(BF16)
    nt = (((1,), (1,)), ((), ()))
    by_re = lax.dot_general(modes, wv[0], nt, preferred_element_type=F32)
    by_im = lax.dot_general(modes, wv[1], nt, preferred_element_type=F32)
    mixed_re = by_re[0:1] - by_im[1:2]
    mixed_im = by_im[0:1] + by_re[1:2]
    mixed = [v[:, t * 128 : t * 128 + 128] for v in (mixed_re, mixed_im) for t in range(2)]
    mixed = jnp.concatenate(mixed + mixed, axis=0).astype(BF16).astype(F32)

    gsend[...] = mixed
    back_copies = []
    for d, z, peer in column:
        copy = pltpu.make_async_remote_copy(
            src_ref=gsend, dst_ref=grecv.at[pl.ds(pl.multiple_of(mz * 8, 8), 8)],
            send_sem=gs_sem.at[d], recv_sem=gr_sem.at[d], device_id=peer, device_id_type=MESH,
        )
        copy.start()
        back_copies.append(copy)
    grecv[pl.ds(pl.multiple_of(mz * 8, 8), 8), :] = mixed
    outer_in.wait()
    for copy in column_copies + row_copies:
        copy.wait_send()
    for copy in reversed(back_copies):
        copy.wait_recv()

    for ri in range(2):
        for h in range(2):
            for t in range(2):
                part = grecv[pl.ds(h * 64 + ri * 2 + t, 8, stride=8), :]
                held[ri * 8 : ri * 8 + 8, pl.ds(h * 256 + t * 128, 128)] = part
    spread[mc, my, batch, half] = held[...].astype(BF16)

    spread_copies = {}
    block = spread.at[mc, my, batch, half]
    for d in steps:
        copy = pltpu.make_async_remote_copy(
            src_ref=block, dst_ref=block, send_sem=bs_sem.at[d], recv_sem=br_sem.at[d],
            device_id=partner(mx + d % 4, my + d // 4), device_id_type=MESH,
        )
        copy.start()
        spread_copies[d] = copy
    for copy in back_copies:
        copy.wait_send()

    pair_copies = []
    for dy in (0, 1, 3, 2):
        for dx in range(4):
            d = dy * 4 + dx
            if d:
                spread_copies[d].wait_recv()
        y = (my + 4 - dy) % 4
        copy = pltpu.make_async_remote_copy(
            src_ref=spread.at[mc, y], dst_ref=spread.at[mc, y], send_sem=as_sem.at[dy],
            recv_sem=ar_sem.at[dy], device_id=sibling, device_id_type=MESH,
        )
        copy.start()
        pair_copies.append(copy)
    for copy in spread_copies.values():
        copy.wait_send()
    for copy in pair_copies:
        copy.wait_recv()
    for copy in pair_copies:
        copy.wait_send()

    for b in range(2):
        modes = spread[:, :, b].reshape(256, WIDTH)
        for h in range(2):
            cells = pl.ds(h * 256, 256)
            spectral = jnp.dot(basis_t[cells, :], modes, preferred_element_type=F32)
            active = gelu(spectral * FIELD_SCALE + pre[b, cells, :]).astype(BF16)
            hidden = jnp.dot(active, inner_t[...], preferred_element_type=F32)
            hidden = gelu(hidden).astype(BF16)
            added = jnp.dot(hidden, outer[...], preferred_element_type=F32)
            out_ref[b, cells, :] = (active.astype(F32) + added).astype(BF16)


def local(grid_field, spectral_weight, skip_weight, inner_weight, outer_weight):
    table = jnp.asarray(local_tables())
    field = grid_field.reshape(2, CELLS, WIDTH)
    weight = jnp.swapaxes(spectral_weight, 2, 3)
    dma = pltpu.SemaphoreType.DMA
    operands = (field, weight, skip_weight, inner_weight, outer_weight, table)
    operands = [pltpu.with_memory_space_constraint(v, pltpu.HBM) for v in operands]
    out = pl.pallas_call(
        body,
        out_shape=jax.ShapeDtypeStruct((2, CELLS, WIDTH), BF16),
        in_specs=[pl.BlockSpec(memory_space=pltpu.HBM)] * 6,
        out_specs=pl.BlockSpec(memory_space=pltpu.VMEM),
        scratch_shapes=[
            pltpu.VMEM((2, CELLS, WIDTH), BF16),
            pltpu.VMEM((2, 256, WIDTH), BF16),
            pltpu.VMEM((WIDTH, WIDTH), BF16),
            pltpu.VMEM((HIDDEN, WIDTH), BF16),
            pltpu.VMEM((HIDDEN, WIDTH), BF16),
            pltpu.VMEM((2, 4, 2, 16, CELLS), F32),
            pltpu.VMEM((2, 4, 2, 16, CELLS), BF16),
            pltpu.VMEM((CELLS, 256), BF16),
            pltpu.VMEM((WIDTH, HIDDEN), BF16),
            pltpu.VMEM((2, CELLS, WIDTH), F32),
            pltpu.VMEM((2, 128, WIDTH), BF16),
            pltpu.VMEM((2, 128, WIDTH), BF16),
            pltpu.VMEM((2, 128, WIDTH), F32),
            pltpu.VMEM((2, 8, 16, WIDTH), BF16),
            pltpu.VMEM((16, 16, WIDTH), BF16),
            pltpu.VMEM((64, 128), F32),
            pltpu.VMEM((16, 8, 128), F32),
            pltpu.VMEM((8, 128), F32),
            pltpu.VMEM((128, 128), F32),
            pltpu.VMEM((16, WIDTH), F32),
            pltpu.VMEM((2, 4, 2, 2, 16, WIDTH), BF16),
            dma((12,)),
            dma((2,)), dma((2,)),
            dma((16,)), dma((16,)),
            dma((16,)), dma((16,)),
            dma((4,)), dma((4,)),
            dma((16,)), dma((16,)),
            dma((16,)), dma((16,)),
            dma((4,)), dma((4,)),
            pltpu.SemaphoreType.REGULAR, pltpu.SemaphoreType.REGULAR, pltpu.SemaphoreType.REGULAR,
        ],
        compiler_params=pltpu.CompilerParams(
            collective_id=0, has_side_effects=True, vmem_limit_bytes=40 << 20
        ),
        cost_estimate=pl.CostEstimate(flops=3_400_000_000, bytes_accessed=7 << 20, transcendentals=1_600_000),
    )(*operands)
    return out.reshape(grid_field.shape)


def solution(mesh):
    in_specs = (P(None, "gx", "gy", None), P("gx", None, None, "gy"), P(), P(), P())
    out_specs = P(None, "gx", "gy", None)
    return jax.shard_map(local, mesh=mesh, in_specs=in_specs, out_specs=out_specs, check_vma=False)
```

time: 55.4 us -> 50.1 us (0.904)
  Pallas kernels: 52.9 us -> 49 us
  local copies, waits for them, and re-layouts: 2.3 us -> 0.97 us
    pallas_call x1, Pallas kernels: 52.9 us -> 49 us  [local(): pl.pallas_call(body, out_shape=jax.ShapeDtypeStruct((2, CELLS, WIDTH), BF...]
    unnamed x1, local copies, waits for them, and re-layouts: 2.3 us -> 0.97 us
where the time goes in v3:
time: 50.1 us; the launch traced here: 50 us
  Pallas kernels  49 us (98%)
  local copies, waits for them, and re-layouts  0.97 us (2%)
    pallas_call x1, Pallas kernels, local(): pl.pallas_call(body, out_shape=jax.ShapeDtypeStruct((2, CELLS, WIDTH), BF...  49 us

profile of v3, /device:TPU:1, one launch (start us, length us, event | category | flops | bytes accessed | tf_op | source)
XLA Modules:
  0.0 50.0 jit_solution(5177821691180343569)
XLA Ops:
  0.0 49.0 %shard_map.64 = bf16[2,512,512]{2,1,0:T(8,128)(2,1)S(1)} custom-call(bf16[2,512,512]{2,1,0:T(8,128)(2,1)} %bitcast.4, bf16[2,2,64,512]{3,2,1,0:T(8,128)(2,1)} %bitcast.5, bf16[512,512]{1,0:T(8,128)(2,1)} %skip_hbm.1, bf16[1024,512]{1,0:T(8,128)(2,1)} %inner_hbm.1, bf16[1024,512]{1,0:T(8,128)(2,1)} %outer_hbm.1, f32[2,4,2,16,512]{4,3,2,1,0:T(8,128)} %constant.2.clone.table_hbm), custom_call_target="tpu_custom_call" | custom-call | flops 3400000000 | bytes 7340032 | tf_op jit(solution)/shard_map/pallas_call | solution.py:320
  49.0 1.0 %copy.8 = bf16[2,16,32,512]{3,2,1,0:T(8,128)(2,1)} copy(bf16[2,16,32,512]{3,2,1,0:T(8,128)(2,1)S(1)} %bitcast.3) | data formatting | bytes 2097152

commit v4 on v3

--- a/solution.py
+++ b/solution.py
@@ -150,8 +150,7 @@
     outer_in = load(outer_hbm, outer)
     second_in.wait()
     make_basis(mc, 4)
-    for b in range(2):
-        own[b] = forward(mc, b)
+    own[0] = forward(mc, 0)
 
     def plane_copy(x, dx, y, dy):
         return pltpu.make_async_remote_copy(
@@ -161,6 +160,8 @@
         )
 
     for b in range(2):
+        if b == 1:
+            own[1] = forward(mc, 1)
         core_copies[b].wait_recv()
         xsend[b] = (own[b] + crecv[b].astype(F32)).astype(BF16).reshape(8, 16, WIDTH)
         if b == 0:
@@ -188,7 +189,6 @@
             src_ref=weight_hbm.at[x % 2], dst_ref=wv.at[:, pl.ds(pl.multiple_of(mx * 64, 64), 64)],
             send_sem=ss_sem.at[d], recv_sem=sr_sem.at[d], device_id=peer, device_id_type=MESH,
         )
-        copy.start()
         row_copies.append(copy)
 
     mine = pl.ds(pl.multiple_of((my * 2 + half) * 16, 16), 16)
@@ -197,6 +197,9 @@
     for copy, d in reversed(list(zip(plane_copies, steps))):
         copy.wait_recv()
         total = total + xrecv[d].astype(F32)
+        if d == 7:
+            for weights in row_copies:
+                weights.start()
     for ri in range(2):
         for t in range(4):
             zsend[pl.ds(ri * 4 + t, 8, stride=8), :] = total[ri * 8 : ri * 8 + 8, t * 128 : t * 128 + 128]
@@ -266,48 +269,68 @@
                 held[ri * 8 : ri * 8 + 8, pl.ds(h * 256 + t * 128, 128)] = part
     spread[mc, my, batch, half] = held[...].astype(BF16)
 
-    spread_copies = {}
     block = spread.at[mc, my, batch, half]
-    for d in steps:
-        copy = pltpu.make_async_remote_copy(
+
+    def arrival(d):
+        return pltpu.make_async_remote_copy(
             src_ref=block, dst_ref=block, send_sem=bs_sem.at[d], recv_sem=br_sem.at[d],
             device_id=partner(mx + d % 4, my + d // 4), device_id_type=MESH,
         )
-        copy.start()
-        spread_copies[d] = copy
+
+    for d in steps:
+        arrival(d).start()
     for copy in back_copies:
         copy.wait_send()
 
-    pair_copies = []
-    for dy in (0, 1, 3, 2):
-        for dx in range(4):
-            d = dy * 4 + dx
-            if d:
-                spread_copies[d].wait_recv()
+    pair_copies = [[], []]
+
+    def pass_on(dy, b):
         y = (my + 4 - dy) % 4
-        copy = pltpu.make_async_remote_copy(
-            src_ref=spread.at[mc, y], dst_ref=spread.at[mc, y], send_sem=as_sem.at[dy],
-            recv_sem=ar_sem.at[dy], device_id=sibling, device_id_type=MESH,
-        )
-        copy.start()
-        pair_copies.append(copy)
-    for copy in spread_copies.values():
+        for x in (2 * b, 2 * b + 1):
+            d = dy * 4 + (mx + 4 - x) % 4
+            if dy:
+                arrival(d).wait_recv()
+            else:
+
+                @pl.when(x != mx)
+                def _():
+                    arrival(d).wait_recv()
+
+        copy = pltpu.make_async_remote_copy(
+            src_ref=spread.at[mc, y, b], dst_ref=spread.at[mc, y, b],
+            send_sem=as_sem.at[dy, b], recv_sem=ar_sem.at[dy, b],
+            device_id=sibling, device_id_type=MESH,
+        )
+        copy.start()
+        pair_copies[b].append(copy)
+
+    def finish(b, h):
+        modes = spread[:, :, b].reshape(256, WIDTH)
+        cells = pl.ds(h * 256, 256)
+        spectral = jnp.dot(basis_t[cells, :], modes, preferred_element_type=F32)
+        active = gelu(spectral * FIELD_SCALE + pre[b, cells, :]).astype(BF16)
+        hidden = jnp.dot(active, inner_t[...], preferred_element_type=F32)
+        hidden = gelu(hidden).astype(BF16)
+        added = jnp.dot(hidden, outer[...], preferred_element_type=F32)
+        out_ref[b, cells, :] = (active.astype(F32) + added).astype(BF16)
+
+    for dy in (0, 1, 3):
+        pass_on(dy, 0)
+        pass_on(dy, 1)
+    pass_on(2, 0)
+    for copy in pair_copies[0]:
+        copy.wait_recv()
+    finish(0, 0)
+    pass_on(2, 1)
+    finish(0, 1)
+    for d in steps:
+        arrival(d).wait_send()
+    for copy in pair_copies[0] + pair_copies[1]:
         copy.wait_send()
-    for copy in pair_copies:
-        copy.wait_recv()
-    for copy in pair_copies:
-        copy.wait_send()
-
-    for b in range(2):
-        modes = spread[:, :, b].reshape(256, WIDTH)
-        for h in range(2):
-            cells = pl.ds(h * 256, 256)
-            spectral = jnp.dot(basis_t[cells, :], modes, preferred_element_type=F32)
-            active = gelu(spectral * FIELD_SCALE + pre[b, cells, :]).astype(BF16)
-            hidden = jnp.dot(active, inner_t[...], preferred_element_type=F32)
-            hidden = gelu(hidden).astype(BF16)
-            added = jnp.dot(hidden, outer[...], preferred_element_type=F32)
-            out_ref[b, cells, :] = (active.astype(F32) + added).astype(BF16)
+    for copy in pair_copies[1]:
+        copy.wait_recv()
+    finish(1, 0)
+    finish(1, 1)
 
 
 def local(grid_field, spectral_weight, skip_weight, inner_weight, outer_weight):
@@ -351,7 +374,7 @@
             dma((4,)), dma((4,)),
             dma((16,)), dma((16,)),
             dma((16,)), dma((16,)),
-            dma((4,)), dma((4,)),
+            dma((4, 2)), dma((4, 2)),
             pltpu.SemaphoreType.REGULAR, pltpu.SemaphoreType.REGULAR, pltpu.SemaphoreType.REGULAR,
         ],
         compiler_params=pltpu.CompilerParams(

time: 50.1 us -> 49.3 us (0.984)
  Pallas kernels: 49 us -> 48.2 us
    pallas_call x1, Pallas kernels: 49 us -> 48.2 us  [local(): pl.pallas_call(body, out_shape=jax.ShapeDtypeStruct((2, CELLS, WIDTH), BF...]
where the time goes in v4:
time: 49.3 us; the launch traced here: 49.2 us
  Pallas kernels  48.2 us (98%)
  local copies, waits for them, and re-layouts  0.97 us (2%)
    pallas_call x1, Pallas kernels, local(): pl.pallas_call(body, out_shape=jax.ShapeDtypeStruct((2, CELLS, WIDTH), BF...  48.2 us

profile of v4, /device:TPU:1, one launch (start us, length us, event | category | flops | bytes accessed | tf_op | source)
XLA Modules:
  0.0 49.2 jit_solution(10266574220094217041)
XLA Ops:
  0.0 48.2 %shard_map.64 = bf16[2,512,512]{2,1,0:T(8,128)(2,1)S(1)} custom-call(bf16[2,512,512]{2,1,0:T(8,128)(2,1)} %bitcast.4, bf16[2,2,64,512]{3,2,1,0:T(8,128)(2,1)} %bitcast.5, bf16[512,512]{1,0:T(8,128)(2,1)} %skip_hbm.1, bf16[1024,512]{1,0:T(8,128)(2,1)} %inner_hbm.1, bf16[1024,512]{1,0:T(8,128)(2,1)} %outer_hbm.1, f32[2,4,2,16,512]{4,3,2,1,0:T(8,128)} %constant.2.clone.table_hbm), custom_call_target="tpu_custom_call" | custom-call | flops 3400000000 | bytes 7340032 | tf_op jit(solution)/shard_map/pallas_call | solution.py:343
  48.2 1.0 %copy.8 = bf16[2,16,32,512]{3,2,1,0:T(8,128)(2,1)} copy(bf16[2,16,32,512]{3,2,1,0:T(8,128)(2,1)S(1)} %bitcast.3) | data formatting | bytes 2097152

commit v5 on v4

--- a/solution.py
+++ b/solution.py
@@ -43,8 +43,8 @@
 
 
 def body(
-    field_hbm, weight_hbm, skip_hbm, inner_hbm, outer_hbm, table_hbm, out_ref,
-    field, wv, skip, inner, outer, table,
+    field_hbm, weight_hbm, skip_hbm, inner_hbm, outer_hbm, table_hbm, out_ref, active_ref, hidden_ref, outer,
+    field, wv, skip, inner, table,
     basis, basis_t, inner_t, pre,
     csend, crecv, own, xsend, xrecv, zsend, zrecv, gsend, grecv, held, spread,
     load_sem, cs_sem, cr_sem, xs_sem, xr_sem, zs_sem, zr_sem, ss_sem, sr_sem,
@@ -198,8 +198,7 @@
         copy.wait_recv()
         total = total + xrecv[d].astype(F32)
         if d == 7:
-            for weights in row_copies:
-                weights.start()
+            row_copies[0].start()
     for ri in range(2):
         for t in range(4):
             zsend[pl.ds(ri * 4 + t, 8, stride=8), :] = total[ri * 8 : ri * 8 + 8, t * 128 : t * 128 + 128]
@@ -213,6 +212,8 @@
         )
         copy.start()
         column_copies.append(copy)
+    row_copies[1].start()
+    row_copies[2].start()
 
     for t in range(4):
         cells = pl.ds(t * 128, 128)
@@ -311,8 +312,12 @@
         active = gelu(spectral * FIELD_SCALE + pre[b, cells, :]).astype(BF16)
         hidden = jnp.dot(active, inner_t[...], preferred_element_type=F32)
         hidden = gelu(hidden).astype(BF16)
-        added = jnp.dot(hidden, outer[...], preferred_element_type=F32)
-        out_ref[b, cells, :] = (active.astype(F32) + added).astype(BF16)
+        if b == 0:
+            added = jnp.dot(hidden, outer[...], preferred_element_type=F32)
+            out_ref[cells, :] = (active.astype(F32) + added).astype(BF16)
+        else:
+            active_ref[cells, :] = active
+            hidden_ref[cells, :] = hidden
 
     for dy in (0, 1, 3):
         pass_on(dy, 0)
@@ -333,6 +338,20 @@
     finish(1, 1)
 
 
+def store(first, active, hidden, outer, out_hbm, second, sems):
+    copies = [pltpu.make_async_copy(first, out_hbm.at[0], sems.at[0])]
+    copies[0].start()
+    for h in range(4):
+        cells = pl.ds(h * 128, 128)
+        added = jnp.dot(hidden[cells, :], outer[...], preferred_element_type=F32)
+        second[cells, :] = (active[cells, :].astype(F32) + added).astype(BF16)
+        copy = pltpu.make_async_copy(second.at[cells], out_hbm.at[1, cells], sems.at[1 + h])
+        copy.start()
+        copies.append(copy)
+    for copy in copies:
+        copy.wait()
+
+
 def local(grid_field, spectral_weight, skip_weight, inner_weight, outer_weight):
     table = jnp.asarray(local_tables())
     field = grid_field.reshape(2, CELLS, WIDTH)
@@ -340,16 +359,20 @@
     dma = pltpu.SemaphoreType.DMA
     operands = (field, weight, skip_weight, inner_weight, outer_weight, table)
     operands = [pltpu.with_memory_space_constraint(v, pltpu.HBM) for v in operands]
-    out = pl.pallas_call(
+    parts = pl.pallas_call(
         body,
-        out_shape=jax.ShapeDtypeStruct((2, CELLS, WIDTH), BF16),
+        out_shape=[
+            jax.ShapeDtypeStruct((CELLS, WIDTH), BF16),
+            jax.ShapeDtypeStruct((CELLS, WIDTH), BF16),
+            jax.ShapeDtypeStruct((CELLS, HIDDEN), BF16),
+            jax.ShapeDtypeStruct((HIDDEN, WIDTH), BF16),
+        ],
         in_specs=[pl.BlockSpec(memory_space=pltpu.HBM)] * 6,
-        out_specs=pl.BlockSpec(memory_space=pltpu.VMEM),
+        out_specs=[pl.BlockSpec(memory_space=pltpu.VMEM)] * 4,
         scratch_shapes=[
             pltpu.VMEM((2, CELLS, WIDTH), BF16),
             pltpu.VMEM((2, 256, WIDTH), BF16),
             pltpu.VMEM((WIDTH, WIDTH), BF16),
-            pltpu.VMEM((HIDDEN, WIDTH), BF16),
             pltpu.VMEM((HIDDEN, WIDTH), BF16),
             pltpu.VMEM((2, 4, 2, 16, CELLS), F32),
             pltpu.VMEM((2, 4, 2, 16, CELLS), BF16),
@@ -382,6 +405,14 @@
         ),
         cost_estimate=pl.CostEstimate(flops=3_400_000_000, bytes_accessed=7 << 20, transcendentals=1_600_000),
     )(*operands)
+    out = pl.pallas_call(
+        store,
+        out_shape=jax.ShapeDtypeStruct((2, CELLS, WIDTH), BF16),
+        in_specs=[pl.BlockSpec(memory_space=pltpu.VMEM)] * 4,
+        out_specs=pl.BlockSpec(memory_space=pltpu.HBM),
+        scratch_shapes=[pltpu.VMEM((CELLS, WIDTH), BF16), dma((5,))],
+        compiler_params=pltpu.CompilerParams(vmem_limit_bytes=16 << 20),
+    )(*parts)
     return out.reshape(grid_field.shape)
 
 

time: 49.3 us -> 49.3 us (level)
  Pallas kernels: 48.2 us -> 49.2 us
  local copies, waits for them, and re-layouts: 0.97 us -> 0 us
    pallas_call x1 -> x2, Pallas kernels: 48.2 us -> 49.2 us  [the longest x1 47.7 us: local(): pl.pallas_call(body, out_shape=[jax.ShapeDtypeStruct((CELLS, WIDTH), BF16...]
    unnamed x1 -> x0, local copies, waits for them, and re-layouts: 0.97 us -> none
where the time goes in v5:
time: 49.3 us; the launch traced here: 49.2 us
  Pallas kernels  49.2 us (100%)
    pallas_call x1, Pallas kernels, local(): pl.pallas_call(body, out_shape=[jax.ShapeDtypeStruct((CELLS, WIDTH), BF16...  47.7 us
    pallas_call x1, Pallas kernels, local(): pl.pallas_call(store, out_shape=jax.ShapeDtypeStruct((2, CELLS, WIDTH), B...  1.43 us

profile of v5, /device:TPU:1, one launch (start us, length us, event | category | flops | bytes accessed | tf_op | source)
XLA Modules:
  0.0 49.2 jit_solution(15299872889205095263)
XLA Ops:
  0.0 47.7 %shard_map.64 = (bf16[512,512]{1,0:T(8,128)(2,1)S(1)}, bf16[512,512]{1,0:T(8,128)(2,1)S(1)}, bf16[512,1024]{1,0:T(8,128)(2,1)S(1)}, bf16[1024,512]{1,0:T(8,128)(2,1)S(1)}) custom-call(bf16[2,512,512]{2,1,0:T(8,128)(2,1)} %bitcast.3, bf16[2,2,64,512]{3,2,1,0:T(8,128)(2,1)} %bitcast.4, bf16[512,512]{1,0:T(8,128)(2,1)} %skip_hbm.1, ...), custom_call_target="tpu_custom_call" | custom-call | flops 3400000000 | bytes 7340032 | tf_op jit(solution)/shard_map/pallas_call | solution.py:362
  47.7 1.4 %shard_map.65 = bf16[2,512,512]{2,1,0:T(8,128)(2,1)} custom-call(bf16[512,512]{1,0:T(8,128)(2,1)S(1)} %get-tuple-element.9.first, bf16[512,512]{1,0:T(8,128)(2,1)S(1)} %get-tuple-element.10.active, bf16[512,1024]{1,0:T(8,128)(2,1)S(1)} %get-tuple-element.11.hidden, bf16[1024,512]{1,0:T(8,128)(2,1)S(1)} %get-tuple-element.12.outer), custom_call_target="tpu_custom_call" | custom-call | tf_op jit(solution)/shard_map/pallas_call | solution.py:408

commit v6 on v4

--- a/solution.py
+++ b/solution.py
@@ -304,33 +304,28 @@
         copy.start()
         pair_copies[b].append(copy)
 
-    def finish(b, h):
+    def finish(b):
         modes = spread[:, :, b].reshape(256, WIDTH)
-        cells = pl.ds(h * 256, 256)
-        spectral = jnp.dot(basis_t[cells, :], modes, preferred_element_type=F32)
-        active = gelu(spectral * FIELD_SCALE + pre[b, cells, :]).astype(BF16)
+        spectral = jnp.dot(basis_t[...], modes, preferred_element_type=F32)
+        active = gelu(spectral * FIELD_SCALE + pre[b]).astype(BF16)
         hidden = jnp.dot(active, inner_t[...], preferred_element_type=F32)
         hidden = gelu(hidden).astype(BF16)
         added = jnp.dot(hidden, outer[...], preferred_element_type=F32)
-        out_ref[b, cells, :] = (active.astype(F32) + added).astype(BF16)
-
-    for dy in (0, 1, 3):
+        out_ref[b] = (active.astype(F32) + added).astype(BF16)
+
+    for dy in (0, 1, 3, 2):
         pass_on(dy, 0)
         pass_on(dy, 1)
-    pass_on(2, 0)
     for copy in pair_copies[0]:
         copy.wait_recv()
-    finish(0, 0)
-    pass_on(2, 1)
-    finish(0, 1)
+    finish(0)
     for d in steps:
         arrival(d).wait_send()
     for copy in pair_copies[0] + pair_copies[1]:
         copy.wait_send()
     for copy in pair_copies[1]:
         copy.wait_recv()
-    finish(1, 0)
-    finish(1, 1)
+    finish(1)
 
 
 def local(grid_field, spectral_weight, skip_weight, inner_weight, outer_weight):

time: 49.3 us -> 49 us (level)
  no operation moved by 1% of the time
where the time goes in v6:
time: 49 us; the launch traced here: 48.9 us
  Pallas kernels  47.9 us (98%)
  local copies, waits for them, and re-layouts  0.97 us (2%)
    pallas_call x1, Pallas kernels, local(): pl.pallas_call(body, out_shape=jax.ShapeDtypeStruct((2, CELLS, WIDTH), BF...  47.9 us

profile of v6, /device:TPU:1, one launch (start us, length us, event | category | flops | bytes accessed | tf_op | source)
XLA Modules:
  0.0 48.9 jit_solution(1395576406724394118)
XLA Ops:
  0.0 47.9 %shard_map.64 = bf16[2,512,512]{2,1,0:T(8,128)(2,1)S(1)} custom-call(bf16[2,512,512]{2,1,0:T(8,128)(2,1)} %bitcast.4, bf16[2,2,64,512]{3,2,1,0:T(8,128)(2,1)} %bitcast.5, bf16[512,512]{1,0:T(8,128)(2,1)} %skip_hbm.1, bf16[1024,512]{1,0:T(8,128)(2,1)} %inner_hbm.1, bf16[1024,512]{1,0:T(8,128)(2,1)} %outer_hbm.1, f32[2,4,2,16,512]{4,3,2,1,0:T(8,128)} %constant.2.clone.table_hbm), custom_call_target="tpu_custom_call" | custom-call | flops 3400000000 | bytes 7340032 | tf_op jit(solution)/shard_map/pallas_call | solution.py:338
  47.9 1.0 %copy.8 = bf16[2,16,32,512]{3,2,1,0:T(8,128)(2,1)} copy(bf16[2,16,32,512]{3,2,1,0:T(8,128)(2,1)S(1)} %bitcast.3) | data formatting | bytes 2097152
